TPU v7x, 512 devices: a whole 4x4x16 slice. The times are simulated.
512 devices in a mesh: inp: 32 (over z_lo, x), tm: 16 (over z_hi, y, core).
Axes of the slice: x: 4, y: 4, z: 16 (z_hi: 2, z_lo: 8; z = z_hi * 8 + z_lo), core: 2. Of those that a mesh axis runs over, the one named last changes fastest.
Arguments:
- voltages: bfloat16 [1024, 524288], P('inp', 'tm'), may hold values from -400 to 400, as said below
Outputs:
- visibilities: bfloat16 [512, 1024, 1024], P(('inp', 'tm'))
Inputs may be any that keep to these rules, and one draw needn't show every extreme that they name: `voltages`: magnitudes stay within about 400.
All inputs are finite; a program needn't handle non-finite values.
Results may differ from a plain program's by a relative error of at most 0.0034.
Values may be sent and summed in bfloat16 or wider, within the bound.
No kernel may reach another device: no remote copies, remote signals or barrier semaphores. Data moves between devices by JAX's collectives and lax.ppermute only.
A program may use at most 64 MiB of HBM per device.

v0:
```python
import math

import jax
import jax.numpy as jnp
from jax import lax
from jax.sharding import PartitionSpec as P

NFFT = 2048
CHANNELS = 512
TAPS = 4


def from_behind(value, axis, steps):
    count = lax.axis_size(axis)
    initial, last = (max(0, -steps), min(count, count - steps))
    return lax.ppermute(value, axis, [(source, source + steps) for source in range(initial, last)])


def filter_window(tap_count, length):
    sample = jnp.arange(tap_count * length, dtype=jnp.float32) + 0.5
    shaped = jnp.sinc(sample / length - tap_count / 2.0)
    tapered = 0.5 - 0.5 * jnp.cos(2.0 * math.pi * sample / (tap_count * length))
    return (shaped * tapered).reshape(tap_count, length)


def phase_table(length, channels):
    sample = jnp.arange(length, dtype=jnp.int32)
    bin_index = length // 2 - channels + jnp.arange(channels, dtype=jnp.int32)
    product = sample[:, None] * bin_index[None, :] % length
    phase_angle = product.astype(jnp.float32) * (2.0 * math.pi / length)
    paired = jnp.stack([jnp.cos(phase_angle), -jnp.sin(phase_angle)], axis=2)
    return paired.reshape(length, 2 * channels).astype(jnp.bfloat16)


def block_product(left_side, right_side):
    return jnp.einsum("rti,rtj->ij", left_side, right_side, preferred_element_type=jnp.float32)


def body(voltages):
    inp_count = lax.axis_size("inp")
    time_count = lax.axis_size("tm")
    local_inputs = voltages.shape[0]
    spec_local = voltages.shape[1] // NFFT
    rim_samples = voltages[:, (spec_local - TAPS + 1) * NFFT :]
    earlier = from_behind(rim_samples, "tm", 1)
    extended = jnp.concatenate([earlier, voltages], axis=1).reshape(
        local_inputs, spec_local + TAPS - 1, NFFT
    )
    window = filter_window(TAPS, NFFT)
    filtered = window[0] * extended[:, 0:spec_local, :].astype(jnp.float32)
    for tap_index in range(1, TAPS):
        filtered = filtered + window[tap_index] * extended[
            :, tap_index : tap_index + spec_local, :
        ].astype(jnp.float32)
    filtered = filtered.astype(jnp.bfloat16)
    spectra = jnp.einsum(
        "isn,nc->csi", filtered, phase_table(NFFT, CHANNELS), preferred_element_type=jnp.float32
    ).astype(jnp.bfloat16)
    per_device = CHANNELS // (inp_count * time_count)
    spectra = spectra.reshape(inp_count, time_count, per_device, 2, spec_local, local_inputs)
    turned = lax.all_to_all(
        lax.all_to_all(spectra, "inp", split_axis=0, concat_axis=5, tiled=True),
        "tm",
        split_axis=1,
        concat_axis=4,
        tiled=True,
    )
    total_spectra = spec_local * time_count
    all_inputs = local_inputs * inp_count
    turned = turned.reshape(per_device, 2, total_spectra, all_inputs)
    upper_mask = jnp.arange(all_inputs)[:, None] <= jnp.arange(all_inputs)[None, :]

    def one_channel(channel_data):
        flipped = jnp.stack([channel_data[1], -channel_data[0]])
        packed = jnp.where(
            upper_mask,
            block_product(channel_data, channel_data),
            block_product(flipped, channel_data),
        )
        mean_power = jnp.diagonal(packed) / total_spectra
        gain_values = 1.0 / jnp.sqrt(mean_power + 1e-06)
        return (packed * gain_values[:, None] * gain_values[None, :] / total_spectra).astype(
            jnp.bfloat16
        )

    return lax.map(one_channel, turned)


def solution(mesh):
    in_specs = (P("inp", "tm"),)
    out_specs = P(("inp", "tm"), None, None)
    return jax.shard_map(body, mesh=mesh, in_specs=in_specs, out_specs=out_specs, check_vma=False)
```

profile of v0, /device:TPU:34, one launch (start us, length us, event | category | flops | bytes accessed | tf_op | source)
XLA Modules:
  0.0 245.3 jit_solution(15864750643465437528)
XLA Ops:
  0.0 1.0 slice.44
  1.0 1.8 collective-permute-start
  2.8 17.0 %cosine_convert_fusion = (bf16[2048,512,1]{1,0,2:T(8,128)(2,1)S(1)}, bf16[2048,512,1]{1,0,2:T(8,128)(2,1)S(1)}) fusion(s32[512]{0:T(512)S(1)} %iota_add_fusion), kind=kLoop, calls=%fused_computation.14 | loop fusion | flops 17825792 | bytes 4196352 | tf_op jit(solution)/shard_map/convert
  19.8 2.3 pad_maximum_fusion
  22.1 11.4 %copy.31 = bf16[2048,512,2]{0,2,1:T(2,128)(2,1)} copy(bf16[2048,512,2]{1,0,2:T(8,128)(2,1)} %pad_maximum_fusion) | data formatting | bytes 8388608 | tf_op jit(solution)/shard_map/stack | solution.py:31
  33.4 0.0 copy-start.1
  33.4 7.3 %convert_element_type.51 = bf16[2048,1024]{0,1:T(8,128)(2,1)} reshape(bf16[2048,512,2]{0,2,1:T(2,128)(2,1)} %copy.31) | data formatting | bytes 8388608 | tf_op jit(solution)/shard_map/convert_element_type | solution.py:32
  40.8 0.2 fusion.29
  41.0 0.0 collective-permute-done
  41.0 0.0 copy-done.1
  41.0 1.7 pad_maximum_fusion.1
  42.6 3.3 %reshape.156 = bf16[32,19,2048]{2,1,0:T(8,128)(2,1)S(1)} reshape(bf16[32,38912]{1,0:T(8,128)(2,1)} %pad_maximum_fusion.1) | data formatting | bytes 4980736 | tf_op jit(solution)/shard_map/reshape | solution.py:46
  46.0 0.0 copy-start
  46.0 2.2 add_convert_fusion
  48.1 0.0 copy-done
  48.2 2.7 %fusion.15 = bf16[1024,16,32]{0,2,1:T(8,128)(2,1)S(1)} fusion(bf16[32,16,2048]{2,1,0:T(8,128)(2,1)S(1)} %add_convert_fusion, bf16[2048,1024]{0,1:T(8,128)(2,1)S(1)} %copy-done), kind=kOutput, calls=%fused_computation.23 | convolution fusion | flops 2148007936 | bytes 7340032 | tf_op jit(solution)/shard_map/isn,nc->csi/dot_general | solution.py:56
  50.9 4.8 %copy.34 = bf16[1024,16,32]{2,1,0:T(8,128)(2,1)} copy(bf16[1024,16,32]{0,2,1:T(8,128)(2,1)S(1)} %fusion.15) | data formatting | bytes 2097152 | tf_op jit(solution)/shard_map/convert_element_type | solution.py:58
  55.7 6.7 %reshape.168 = bf16[32,2,8192]{2,1,0:T(2,128)(2,1)S(1)} reshape(bf16[32,1,16,2,16,32]{5,4,3,2,1,0:T(8,128)(2,1)} %bitcast.50) | data formatting | bytes 2097152
  62.3 64.8 %all_to_all.33 = bf16[32,2,8192]{2,1,0:T(2,128)(2,1)S(1)} all-to-all(bf16[32,2,8192]{2,1,0:T(2,128)(2,1)S(1)} %reshape.168), channel_id=1, replica_groups=mesh['inp'=32,'tm'=16] {'inp'}, dimensions={0} | all-to-all | bytes 2097152 | tf_op jit(solution)/shard_map/all_to_all | solution.py:62
  127.2 3.5 %reshape.169 = bf16[32,1,16,2,16,32]{5,4,3,2,1,0:T(8,128)(2,1)} reshape(bf16[32,2,8192]{2,1,0:T(2,128)(2,1)S(1)} %all_to_all.33) | data formatting | bytes 2097152
  130.7 3.0 %bitcast_bitcast_fusion = bf16[1,16,1,2,16,32,32]{6,4,3,1,5,2,0:T(8,128)(2,1)S(1)} fusion(bf16[32,1,16,2,16,32]{5,4,3,2,1,0:T(8,128)(2,1)} %reshape.169), kind=kLoop, calls=%fused_computation.62 | loop fusion | bytes 2097152 | tf_op jit(solution)/shard_map/all_to_all | solution.py:62
  133.7 6.8 %copy.36 = bf16[1,16,1,2,16,32,32]{6,5,4,3,1,2,0:T(8,128)(2,1)} copy(bf16[1,16,1,2,16,32,32]{6,4,3,1,5,2,0:T(8,128)(2,1)S(1)} %bitcast_bitcast_fusion) | data formatting | bytes 2097152 | tf_op jit(solution)/shard_map/all_to_all | solution.py:62
  140.5 7.0 %all_to_all.27 = bf16[1,16,1,2,16,1024]{5,4,3,1,2,0:T(8,128)(2,1)} reshape(bf16[1,16,1,2,16,32,32]{6,5,4,3,1,2,0:T(8,128)(2,1)} %copy.36) | data formatting | bytes 2097152 | tf_op jit(solution)/shard_map/all_to_all | solution.py:62
  147.5 10.9 %all-to-all-start.1 = ((bf16[1,16,1,2,16,1024]{5,4,3,2,0,1:T(8,128)(2,1)}), bf16[1,16,1,2,16,1024]{5,4,3,2,0,1:T(8,128)(2,1)S(1)}, u32[]{:S(2)}, u32[]{:S(2)}) async-start(bf16[1,16,1,2,16,1024]{5,4,3,2,0,1:T(8,128)(2,1)} %bitcast.6), calls=%async_computation.1 | async-start | bytes 2097152 | tf_op jit(solution)/shard_map/all_to_all | solution.py:61
  158.4 58.9 %all-to-all-done.1 = bf16[1,16,1,2,16,1024]{5,4,3,2,0,1:T(8,128)(2,1)S(1)} async-done(((bf16[1,16,1,2,16,1024]{5,4,3,2,0,1:T(8,128)(2,1)}), bf16[1,16,1,2,16,1024]{5,4,3,2,0,1:T(8,128)(2,1)S(1)}, u32[]{:S(2)}, u32[]{:S(2)}) %all-to-all-start.1) | async-done | bytes 1048608 | tf_op jit(solution)/shard_map/all_to_all | solution.py:61
  217.3 0.1 copy.56
  217.4 0.9 fusion.40
  218.3 0.2 copy.39
  218.5 1.2 copy.40
  219.7 1.3 fusion.23
  221.0 3.2 %bitcast_select_fusion = f32[1024,1024]{1,0:T(8,128)} fusion(f32[1024,1024,1,1]{1,0,3,2:T(8,128)S(1)} %fusion.23, bf16[2,256,1024]{2,1,0:T(8,128)(2,1)S(1)} %bitcast.52, bf16[1,256,1024]{1,2,0:T(8,128)(2,1)S(1)} %copy.40, bf16[1,256,1024]{1,2,0:T(8,128)(2,1)S(1)} %copy.39), kind=kOutput, calls=%fused_computation.8 | convolution fusion | flops 1076363264 | bytes 10485760 | tf_op jit(solution)/shard_map/while/body/eval_jaxpr/rti,rtj->ij/dot_general | solution.py:36
  224.3 17.0 %gather_fusion = f32[1024]{0:T(1024)S(1)} fusion(f32[1024,1024]{1,0:T(8,128)} %bitcast_select_fusion, s32[1024]{0:T(1024)S(1)} %bitcast.49), kind=kCustom, calls=%fused_computation | custom fusion | bytes 16384 | tf_op jit(solution)/shard_map/while/body/eval_jaxpr/jit(diagonal)/cond/branch_0_fun/gather | solution.py:80
  241.3 4.0 %fusion.8 = bf16[1,1024,1024]{2,1,0:T(8,128)(2,1)} fusion(f32[1024,1024]{1,0:T(8,128)} %bitcast_select_fusion, f32[1024]{0:T(1024)S(1)} %add_rsqrt_fusion), kind=kLoop, calls=%fused_computation.20 | loop fusion | flops 4194304 | bytes 6295552 | tf_op jit(solution)/shard_map/while/body/jit(dynamic_update_index_in_dim)/broadcast_in_dim | solution.py:86
  (4 shorter events, 0.0 us)
Async XLA Ops:
  1.0 39.9 %collective-permute-start = (bf16[32,6144]{1,0:T(8,128)(2,1)S(1)}, bf16[32,6144]{1,0:T(8,128)(2,1)S(1)}, u32[]{:S(2)}, u32[]{:S(2)}) collective-permute-start(bf16[32,6144]{1,0:T(8,128)(2,1)S(1)} %slice.44), channel_id=1, source_target_pairs={{0,1},{1,2},{2,3},{3,4},{4,5},{5,6},{6,7},{7,8},{8,9},{9,10},{10,1... | collective-permute-start | bytes 1179656 | tf_op jit(solution)/shard_map/ppermute | solution.py:16
  33.4 7.5 %copy-start.1 = (bf16[32,32768]{1,0:T(8,128)(2,1)S(1)}, bf16[32,32768]{1,0:T(8,128)(2,1)}, u32[]{:S(2)}) copy-start(bf16[32,32768]{1,0:T(8,128)(2,1)} %param.1) | copy-start | bytes 6291460
  46.0 2.2 copy-start
  147.5 69.8 %all-to-all-start.1 = ((bf16[1,16,1,2,16,1024]{5,4,3,2,0,1:T(8,128)(2,1)}), bf16[1,16,1,2,16,1024]{5,4,3,2,0,1:T(8,128)(2,1)S(1)}, u32[]{:S(2)}, u32[]{:S(2)}) async-start(bf16[1,16,1,2,16,1024]{5,4,3,2,0,1:T(8,128)(2,1)} %bitcast.6), calls=%async_computation.1 | async-start | bytes 2097152 | tf_op jit(solution)/shard_map/all_to_all | solution.py:61
where the time goes:
time: 247 us; the launch traced here: 245 us
  local copies, waits for them, and re-layouts  73.3 us (30%)
  blocking collectives  64.8 us (26%)
  waiting for transfers between devices  58.9 us (24%)
  other arithmetic  28.2 us (11%)
  starting transfers between devices  12.7 us (5%)
  matrix products  7.21 us (3%)
    all_to_all x1, blocking collectives, body(): lax.all_to_all(spectra, 'inp', split_axis=0, concat_axis=5, tiled=True)  64.8 us
    all_to_all x1, waiting for transfers between devices, body(): lax.all_to_all(lax.all_to_all(spectra, 'inp', split_axis=0, concat_axis=5...  58.9 us
    gather x1, local copies, waits for them, and re-layouts, one_channel(): mean_power = jnp.diagonal(packed) / total_spectra  17 us
    another operation x1, other arithmetic  17 us
    all_to_all x3, local copies, waits for them, and re-layouts, body(): lax.all_to_all(spectra, 'inp', split_axis=0, concat_axis=5, tiled=True)  16.8 us
    another operation x1, local copies, waits for them, and re-layouts, phase_table(): paired = jnp.stack([jnp.cos(phase_angle), -jnp.sin(phase_angle)], axis=2)  11.4 us
    all_to_all x1, starting transfers between devices, body(): lax.all_to_all(lax.all_to_all(spectra, 'inp', split_axis=0, concat_axis=5...  10.9 us
    unnamed x6, local copies, waits for them, and re-layouts  10.2 us
  transfers between devices with their start and end apart: 2, of which 1 were waited for; matrix products, arithmetic and copies ran while one was open for 16% of the time, Pallas kernels for 0%

commit v1 on v0

v1 whole, which is shorter than its diff:
```python
import math

import jax
import jax.numpy as jnp
import ml_dtypes
import numpy as np
from jax import lax
from jax.experimental import pallas as pl
from jax.experimental.pallas import tpu as pltpu
from jax.sharding import PartitionSpec as P

NFFT = 2048
CHANNELS = 512
TAPS = 4
LANES = 128


def filter_window():
    sample = np.arange(TAPS * NFFT, dtype=np.float64) + 0.5
    shaped = np.sinc(sample / NFFT - TAPS / 2.0)
    tapered = 0.5 - 0.5 * np.cos(2.0 * math.pi * sample / (TAPS * NFFT))
    return (shaped * tapered).reshape(TAPS, NFFT).astype(np.float32)


def phase_rows(block):
    sample = np.arange(NFFT, dtype=np.int64)
    bin_index = NFFT // 2 - CHANNELS + np.arange(CHANNELS, dtype=np.int64)
    product = (bin_index[:, None] * sample[None, :]) % NFFT
    angle = (product.astype(np.float32) * np.float32(2.0 * math.pi / NFFT)).astype(np.float64)
    paired = np.stack([np.cos(angle), -np.sin(angle)]).astype(np.float32)
    paired = paired.reshape(2, CHANNELS // block, block, NFFT).transpose(1, 0, 2, 3)
    return paired.reshape(2 * CHANNELS, NFFT).astype(ml_dtypes.bfloat16)


def front_kernel(spec_local, slots, v_ref, w_ref, tab_ref, out_ref, filt, stage):
    inputs = v_ref.shape[0]
    block = tab_ref.shape[0] // 2
    tiles = slots * inputs // LANES

    @pl.when(pl.program_id(0) == 0)
    def _():
        @pl.loop(0, NFFT // LANES)
        def _(q):
            off = pl.multiple_of(q * LANES, LANES)
            weights = [w_ref[k : k + 1, pl.ds(off, LANES)] for k in range(TAPS)]
            rows = [
                v_ref[:, pl.ds(pl.multiple_of(s * NFFT + off, LANES), LANES)].astype(jnp.float32)
                for s in range(spec_local)
            ]
            for j in range(slots):
                total = None
                for k in range(TAPS):
                    s = j + k - TAPS + 1
                    if 0 <= s < spec_local:
                        term = weights[k] * rows[s]
                        total = term if total is None else total + term
                if total is None:
                    total = jnp.zeros((inputs, LANES), jnp.float32)
                filt[j * inputs : (j + 1) * inputs, pl.ds(off, LANES)] = total.astype(jnp.bfloat16)

    acc = lax.dot_general(
        tab_ref[...], filt[...], (((1,), (1,)), ((), ())), preferred_element_type=jnp.float32
    )
    for t in range(tiles):
        for r in range(2):
            stage[pl.ds(2 * t + r, block, stride=2 * tiles), :] = acc[
                r * block : (r + 1) * block, t * LANES : (t + 1) * LANES
            ]
    out_ref[...] = stage[...].astype(jnp.bfloat16)


def back_kernel(groups, total_spectra, x_ref, fold_ref, perm_ref, out_ref, a_ref, at_ref, bt_ref, stage, sems):
    per_group = LANES * 4
    inputs = groups * LANES
    depth = a_ref.shape[0]
    half_sign = jnp.where(lax.broadcasted_iota(jnp.int32, (1, LANES), 1) < LANES // 2, 1.0, -1.0)
    for g in range(groups):
        joined = jnp.concatenate([x_ref[4 * g + i] for i in range(4)], axis=1)
        spectra = jnp.dot(fold_ref[...], joined, preferred_element_type=jnp.float32).astype(jnp.bfloat16)
        turned = jnp.dot(spectra, perm_ref[...], preferred_element_type=jnp.float32).astype(jnp.bfloat16)
        flipped = lax.dot_general(
            perm_ref[...], spectra, (((1,), (1,)), ((), ())), preferred_element_type=jnp.float32
        )
        swapped = pltpu.roll(flipped, LANES // 2, 1) * half_sign
        flipped = flipped.astype(jnp.bfloat16)
        swapped = swapped.astype(jnp.bfloat16)
        for u in range(4):
            rows = slice(u * LANES, (u + 1) * LANES)
            cols = slice(g * LANES, (g + 1) * LANES)
            a_ref[rows, cols] = turned[:, rows]
            at_ref[cols, rows] = flipped[rows, :]
            bt_ref[cols, rows] = swapped[rows, :]
    scale = 1.0 / total_spectra
    wide = a_ref[...].astype(jnp.float32)
    row_gain = lax.rsqrt(jnp.sum(wide * wide, axis=0, keepdims=True) * scale + 1e-06) * scale
    size = inputs // 4
    copies = []
    for i in range(4):
        rows = slice(i * size, (i + 1) * size)
        tall = at_ref[rows, :].astype(jnp.float32)
        col_gain = lax.rsqrt(jnp.sum(tall * tall, axis=1, keepdims=True) * scale + 1e-06)
        upper = jnp.dot(at_ref[rows, :], a_ref[:, i * size :], preferred_element_type=jnp.float32)
        lower = jnp.dot(bt_ref[rows, :], a_ref[:, : (i + 1) * size], preferred_element_type=jnp.float32)
        keep = lax.broadcasted_iota(jnp.int32, (size, size), 0) <= lax.broadcasted_iota(jnp.int32, (size, size), 1)
        for j in range(4):
            cols = slice(j * size, (j + 1) * size)
            if j < i:
                part = lower[:, cols]
            elif j > i:
                part = upper[:, (j - i) * size : (j - i + 1) * size]
            else:
                part = jnp.where(keep, upper[:, :size], lower[:, cols])
            stage[rows, cols] = (part * col_gain * row_gain[:, cols]).astype(jnp.bfloat16)
        copies.append(pltpu.make_async_copy(stage.at[rows, :], out_ref.at[0, rows, :], sems.at[i]))
        copies[-1].start()
    for copy in copies:
        copy.wait()


def fold_rows(time_count, tiles, tiles_local):
    fold = np.zeros((2, time_count, tiles_local, time_count, tiles, 2), np.float32)
    for r in range(2):
        for t in range(time_count):
            for u in range(tiles_local):
                fold[r, t, u, t, u, r] = 1.0
            if t:
                fold[r, t, 0, t - 1, tiles_local, r] = 1.0
    return fold.reshape(2 * time_count * tiles_local, -1).astype(ml_dtypes.bfloat16)


def lane_turn():
    turn = np.zeros((4, 4, 32, 4, 4, 32), np.float32)
    for i in range(4):
        for u in range(4):
            for a in range(32):
                turn[i, u, a, u, i, a] = 1.0
    return turn.reshape(512, 512).astype(ml_dtypes.bfloat16)


def body(voltages):
    inp_count = lax.axis_size("inp")
    time_count = lax.axis_size("tm")
    devices = inp_count * time_count
    local_inputs = voltages.shape[0]
    spec_local = voltages.shape[1] // NFFT
    slots = spec_local + 4
    tiles = slots * local_inputs // LANES
    tiles_local = spec_local * local_inputs // LANES
    block = 128
    steps = CHANNELS // block
    sent = pl.pallas_call(
        lambda *refs: front_kernel(spec_local, slots, *refs),
        grid=(steps,),
        in_specs=[
            pl.BlockSpec(voltages.shape, lambda i: (0, 0)),
            pl.BlockSpec((TAPS, NFFT), lambda i: (0, 0)),
            pl.BlockSpec((2 * block, NFFT), lambda i: (i, 0)),
        ],
        out_specs=pl.BlockSpec((block * 2 * tiles, LANES), lambda i: (i, 0)),
        out_shape=jax.ShapeDtypeStruct((CHANNELS * 2 * tiles, LANES), jnp.bfloat16),
        scratch_shapes=[
            pltpu.VMEM((slots * local_inputs, NFFT), jnp.bfloat16),
            pltpu.VMEM((block * 2 * tiles, LANES), jnp.float32),
        ],
        compiler_params=pltpu.CompilerParams(vmem_limit_bytes=24 * 1024 * 1024),
    )(voltages, jnp.asarray(filter_window()), jnp.asarray(phase_rows(block)))
    got = lax.all_to_all(
        sent.reshape(devices, tiles, 2, LANES), ("inp", "tm"), split_axis=0, concat_axis=0, tiled=True
    )
    got = got.reshape(inp_count, time_count * tiles * 2, LANES)
    total_spectra = spec_local * time_count
    inputs = inp_count * local_inputs
    depth = 2 * total_spectra
    vmem = pl.BlockSpec(memory_space=pltpu.VMEM)
    return pl.pallas_call(
        lambda *refs: back_kernel(inputs // LANES, total_spectra, *refs),
        in_specs=[vmem] * 3,
        out_specs=pl.BlockSpec(memory_space=pl.ANY),
        out_shape=jax.ShapeDtypeStruct((1, inputs, inputs), jnp.bfloat16),
        scratch_shapes=[
            pltpu.VMEM((depth, inputs), jnp.bfloat16),
            pltpu.VMEM((inputs, depth), jnp.bfloat16),
            pltpu.VMEM((inputs, depth), jnp.bfloat16),
            pltpu.VMEM((inputs, inputs), jnp.bfloat16),
            pltpu.SemaphoreType.DMA((4,)),
        ],
        compiler_params=pltpu.CompilerParams(vmem_limit_bytes=24 * 1024 * 1024),
    )(got, jnp.asarray(fold_rows(time_count, tiles, tiles_local)), jnp.asarray(lane_turn()))


def solution(mesh):
    in_specs = (P("inp", "tm"),)
    out_specs = P(("inp", "tm"), None, None)
    return jax.shard_map(body, mesh=mesh, in_specs=in_specs, out_specs=out_specs, check_vma=False)
```

time: 247 us -> 109 us (0.44)
  the two profiles are of different devices: /device:TPU:34 before, /device:TPU:1 now
where the time goes in v1:
time: 109 us
  blocking collectives  94.2 us (86%)
  Pallas kernels  10.4 us (10%)
  local copies, waits for them, and re-layouts  4.55 us (4%)
    all_to_all x1, blocking collectives, body(): lax.all_to_all(sent.reshape(devices, tiles, 2, LANES), ('inp', 'tm'), spl...  94.2 us
    pallas_call x1, Pallas kernels, body(): pl.pallas_call(lambda *refs: front_kernel(spec_local, slots, *refs), grid...  5.56 us
    pallas_call x1, Pallas kernels, body(): pl.pallas_call(lambda *refs: back_kernel(inputs // LANES, total_spectra,...  4.85 us
    unnamed x10, local copies, waits for them, and re-layouts  4.55 us

profile of v1, /device:TPU:1, one launch (start us, length us, event | category | flops | bytes accessed | tf_op | source)
XLA Modules:
  0.0 109.2 jit_solution(5423908079202357165)
XLA Ops:
  0.0 0.0 copy-start
  0.0 2.2 %copy-done = bf16[1024,2048]{1,0:T(8,128)(2,1)S(1)} copy-done((bf16[1024,2048]{1,0:T(8,128)(2,1)S(1)}, bf16[1024,2048]{1,0:T(8,128)(2,1)}, u32[]{:S(2)}) %copy-start) | copy-done | bytes 4194328
  2.2 0.0 copy-start.1
  2.2 1.6 %copy-done.1 = bf16[32,32768]{1,0:T(8,128)(2,1)S(1)} copy-done((bf16[32,32768]{1,0:T(8,128)(2,1)S(1)}, bf16[32,32768]{1,0:T(8,128)(2,1)}, u32[]{:S(2)}) %copy-start.1) | copy-done | bytes 2097176
  3.8 0.0 copy-start.4
  3.8 0.8 copy-done.4
  4.5 5.6 %shard_map.55 = bf16[5120,128]{1,0:T(8,128)(2,1)S(1)} custom-call(bf16[32,32768]{1,0:T(8,128)(2,1)S(1)} %copy-done.1, f32[4,2048]{1,0:T(4,128)S(1)} %copy-done.4, bf16[1024,2048]{1,0:T(8,128)(2,1)S(1)} %copy-done), custom_call_target="tpu_custom_call" | custom-call | tf_op jit(solution)/shard_map/pallas_call | solution.py:151
  10.1 0.0 copy-start.2
  10.1 0.0 copy-start.3
  10.1 94.2 %all_to_all.5 = bf16[512,5,2,128]{3,2,1,0:T(2,128)(2,1)S(1)} all-to-all(bf16[512,5,2,128]{3,2,1,0:T(2,128)(2,1)S(1)} %bitcast.3), channel_id=1, replica_groups=mesh['inp'=32,'tm'=16] {'inp','tm'}, dimensions={0} | all-to-all | bytes 2621440 | tf_op jit(solution)/shard_map/all_to_all | solution.py:167
  104.3 0.0 copy-done.2
  104.3 0.0 copy-done.3
  104.3 4.8 %shard_map.56 = bf16[1,1024,1024]{2,1,0:T(8,128)(2,1)} custom-call(bf16[32,160,128]{2,1,0:T(8,128)(2,1)S(1)} %bitcast.2, bf16[128,160]{1,0:T(8,128)(2,1)S(1)} %copy-done.3, bf16[512,512]{1,0:T(8,128)(2,1)S(1)} %copy-done.2), custom_call_target="tpu_custom_call" | custom-call | tf_op jit(solution)/shard_map/pallas_call | solution.py:175
Async XLA Ops:
  0.0 2.2 %copy-start = (bf16[1024,2048]{1,0:T(8,128)(2,1)S(1)}, bf16[1024,2048]{1,0:T(8,128)(2,1)}, u32[]{:S(2)}) copy-start(bf16[1024,2048]{1,0:T(8,128)(2,1)} %constant.9.clone.refs_2_) | copy-start | bytes 12582916
  2.2 1.6 %copy-start.1 = (bf16[32,32768]{1,0:T(8,128)(2,1)S(1)}, bf16[32,32768]{1,0:T(8,128)(2,1)}, u32[]{:S(2)}) copy-start(bf16[32,32768]{1,0:T(8,128)(2,1)} %refs_0_.1) | copy-start | bytes 6291460
  3.8 0.8 copy-start.4
  10.1 94.2 %copy-start.2 = (bf16[512,512]{1,0:T(8,128)(2,1)S(1)}, bf16[512,512]{1,0:T(8,128)(2,1)}, u32[]{:S(2)}) copy-start(bf16[512,512]{1,0:T(8,128)(2,1)} %constant.11.clone.refs_2_) | copy-start | bytes 1572868
  10.1 94.2 %copy-start.3 = (bf16[128,160]{1,0:T(8,128)(2,1)S(1)}, bf16[128,160]{1,0:T(8,128)(2,1)}, u32[]{:S(2)}) copy-start(bf16[128,160]{1,0:T(8,128)(2,1)} %constant.10.clone.refs_1_) | copy-start | bytes 122884

commit v2 on v1

--- a/solution.py
+++ b/solution.py
@@ -23,50 +23,103 @@
 
 
 def phase_rows(block):
-    sample = np.arange(NFFT, dtype=np.int64)
+    sample = np.arange(NFFT // 4, dtype=np.int64)
     bin_index = NFFT // 2 - CHANNELS + np.arange(CHANNELS, dtype=np.int64)
     product = (bin_index[:, None] * sample[None, :]) % NFFT
     angle = (product.astype(np.float32) * np.float32(2.0 * math.pi / NFFT)).astype(np.float64)
     paired = np.stack([np.cos(angle), -np.sin(angle)]).astype(np.float32)
-    paired = paired.reshape(2, CHANNELS // block, block, NFFT).transpose(1, 0, 2, 3)
-    return paired.reshape(2 * CHANNELS, NFFT).astype(ml_dtypes.bfloat16)
-
-
-def front_kernel(spec_local, slots, v_ref, w_ref, tab_ref, out_ref, filt, stage):
+    paired = paired.reshape(2, block, 4, NFFT // 4).transpose(2, 0, 1, 3)
+    return paired.reshape(2 * CHANNELS, NFFT // 4).astype(ml_dtypes.bfloat16)
+
+
+def front_kernel(v_hbm, w_hbm, t_hbm, out_hbm, v_ref, w_ref, t_ref, filt, stage, packed, v_sem, w_sem, t_sem, o_sem):
     inputs = v_ref.shape[0]
-    block = tab_ref.shape[0] // 2
-    tiles = slots * inputs // LANES
-
-    @pl.when(pl.program_id(0) == 0)
-    def _():
-        @pl.loop(0, NFFT // LANES)
-        def _(q):
-            off = pl.multiple_of(q * LANES, LANES)
-            weights = [w_ref[k : k + 1, pl.ds(off, LANES)] for k in range(TAPS)]
-            rows = [
-                v_ref[:, pl.ds(pl.multiple_of(s * NFFT + off, LANES), LANES)].astype(jnp.float32)
-                for s in range(spec_local)
-            ]
-            for j in range(slots):
-                total = None
-                for k in range(TAPS):
-                    s = j + k - TAPS + 1
-                    if 0 <= s < spec_local:
-                        term = weights[k] * rows[s]
-                        total = term if total is None else total + term
-                if total is None:
-                    total = jnp.zeros((inputs, LANES), jnp.float32)
-                filt[j * inputs : (j + 1) * inputs, pl.ds(off, LANES)] = total.astype(jnp.bfloat16)
-
-    acc = lax.dot_general(
-        tab_ref[...], filt[...], (((1,), (1,)), ((), ())), preferred_element_type=jnp.float32
-    )
-    for t in range(tiles):
-        for r in range(2):
-            stage[pl.ds(2 * t + r, block, stride=2 * tiles), :] = acc[
-                r * block : (r + 1) * block, t * LANES : (t + 1) * LANES
-            ]
-    out_ref[...] = stage[...].astype(jnp.bfloat16)
+    spec_local = v_ref.shape[1] // NFFT
+    per_tile = LANES // inputs
+    tiles = filt.shape[0] // LANES
+    block = t_ref.shape[0] // 8
+    parts = v_sem.shape[0]
+    width = v_ref.shape[1] // parts
+    fetch_v = [
+        pltpu.make_async_copy(
+            v_hbm.at[:, i * width : (i + 1) * width], v_ref.at[:, i * width : (i + 1) * width], v_sem.at[i]
+        )
+        for i in range(parts)
+    ]
+    fetch_w = pltpu.make_async_copy(w_hbm, w_ref, w_sem)
+    fetch_t = pltpu.make_async_copy(t_hbm, t_ref, t_sem)
+    fetch_w.start()
+    fetch_v[0].start()
+    fetch_v[1].start()
+    fetch_t.start()
+    fetch_v[2].start()
+    fetch_v[3].start()
+    fetch_w.wait()
+
+    def filter_tiles(first, last, off):
+        weights = [w_ref[k : k + 1, pl.ds(off, LANES)] for k in range(TAPS)]
+        slots = range(first * per_tile, last * per_tile)
+        need = sorted({j + k - TAPS + 1 for j in slots for k in range(TAPS)} & set(range(spec_local)))
+        rows = {
+            s: v_ref[:, pl.ds(pl.multiple_of(s * NFFT + off, LANES), LANES)].astype(jnp.float32) for s in need
+        }
+        for j in slots:
+            total = None
+            for k in range(TAPS):
+                s = j + k - TAPS + 1
+                if s in rows:
+                    term = weights[k] * rows[s]
+                    total = term if total is None else total + term
+            if total is None:
+                total = jnp.zeros((inputs, LANES), jnp.float32)
+            filt[j * inputs : (j + 1) * inputs, pl.ds(off, LANES)] = total.astype(jnp.bfloat16)
+
+    def phases(residue):
+        real = t_ref[2 * residue * block : (2 * residue + 1) * block, :]
+        imag = t_ref[(2 * residue + 1) * block : (2 * residue + 2) * block, :]
+        turns = [(real, imag), (imag, -real), (-real, -imag), (-imag, real)]
+        quarters = [turns[(residue * q) % 4] for q in range(4)]
+        return jnp.concatenate([jnp.concatenate([part[r] for part in quarters], axis=1) for r in range(2)], axis=0)
+
+    def transform(first, last):
+        for residue in range(4):
+            acc = lax.dot_general(
+                phases(residue),
+                filt[first * LANES : last * LANES, :],
+                (((1,), (1,)), ((), ())),
+                preferred_element_type=jnp.float32,
+            )
+            for t in range(first, last):
+                for r in range(2):
+                    stage[pl.ds(residue * 2 * tiles + 2 * t + r, block, stride=8 * tiles), :] = acc[
+                        r * block : (r + 1) * block, (t - first) * LANES : (t - first + 1) * LANES
+                    ]
+
+    fetch_v[0].wait()
+    fetch_v[1].wait()
+
+    @pl.loop(0, NFFT // LANES)
+    def _(q):
+        filter_tiles(0, 2, pl.multiple_of(q * LANES, LANES))
+
+    fetch_v[2].wait()
+    fetch_v[3].wait()
+    fetch_t.wait()
+    transform(0, 2)
+    for q in range(NFFT // LANES):
+        filter_tiles(2, 4, q * LANES)
+    for q in range(NFFT // LANES):
+        filter_tiles(4, tiles, q * LANES)
+    transform(2, tiles)
+    size = packed.shape[0] // 4
+    stores = []
+    for i in range(4):
+        rows = slice(i * size, (i + 1) * size)
+        packed[rows, :] = stage[rows, :].astype(jnp.bfloat16)
+        stores.append(pltpu.make_async_copy(packed.at[rows, :], out_hbm.at[rows, :], o_sem.at[i]))
+        stores[-1].start()
+    for store in stores:
+        store.wait()
 
 
 def back_kernel(groups, total_spectra, x_ref, fold_ref, perm_ref, out_ref, a_ref, at_ref, bt_ref, stage, sems):
@@ -146,23 +199,27 @@
     slots = spec_local + 4
     tiles = slots * local_inputs // LANES
     tiles_local = spec_local * local_inputs // LANES
-    block = 128
-    steps = CHANNELS // block
+    block = CHANNELS // 4
+    rows = CHANNELS * 2 * tiles
+    hbm = pl.BlockSpec(memory_space=pl.ANY)
     sent = pl.pallas_call(
-        lambda *refs: front_kernel(spec_local, slots, *refs),
-        grid=(steps,),
-        in_specs=[
-            pl.BlockSpec(voltages.shape, lambda i: (0, 0)),
-            pl.BlockSpec((TAPS, NFFT), lambda i: (0, 0)),
-            pl.BlockSpec((2 * block, NFFT), lambda i: (i, 0)),
+        front_kernel,
+        in_specs=[hbm] * 3,
+        out_specs=hbm,
+        out_shape=jax.ShapeDtypeStruct((rows, LANES), jnp.bfloat16),
+        scratch_shapes=[
+            pltpu.VMEM(voltages.shape, jnp.bfloat16),
+            pltpu.VMEM((TAPS, NFFT), jnp.float32),
+            pltpu.VMEM((2 * CHANNELS, NFFT // 4), jnp.bfloat16),
+            pltpu.VMEM((slots * local_inputs, NFFT), jnp.bfloat16),
+            pltpu.VMEM((rows, LANES), jnp.float32),
+            pltpu.VMEM((rows, LANES), jnp.bfloat16),
+            pltpu.SemaphoreType.DMA((4,)),
+            pltpu.SemaphoreType.DMA,
+            pltpu.SemaphoreType.DMA,
+            pltpu.SemaphoreType.DMA((4,)),
         ],
-        out_specs=pl.BlockSpec((block * 2 * tiles, LANES), lambda i: (i, 0)),
-        out_shape=jax.ShapeDtypeStruct((CHANNELS * 2 * tiles, LANES), jnp.bfloat16),
-        scratch_shapes=[
-            pltpu.VMEM((slots * local_inputs, NFFT), jnp.bfloat16),
-            pltpu.VMEM((block * 2 * tiles, LANES), jnp.float32),
-        ],
-        compiler_params=pltpu.CompilerParams(vmem_limit_bytes=24 * 1024 * 1024),
+        compiler_params=pltpu.CompilerParams(vmem_limit_bytes=60 * 1024 * 1024),
     )(voltages, jnp.asarray(filter_window()), jnp.asarray(phase_rows(block)))
     got = lax.all_to_all(
         sent.reshape(devices, tiles, 2, LANES), ("inp", "tm"), split_axis=0, concat_axis=0, tiled=True

time: 109 us -> 107 us (0.982)
  local copies, waits for them, and re-layouts: 4.55 us -> 0.01 us
  Pallas kernels: 10.4 us -> 12 us
    unnamed x10 -> x4, local copies, waits for them, and re-layouts: 4.55 us -> 0.01 us
    pallas_call x1, Pallas kernels: 5.56 us -> 7.15 us  [body(): pl.pallas_call(front_kernel, in_specs=[hbm] * 3, out_specs=hbm, out_shape...]
where the time goes in v2:
time: 107 us; the launch traced here: 106 us
  blocking collectives  94.4 us (88%)
  Pallas kernels  12 us (11%)
    all_to_all x1, blocking collectives, body(): lax.all_to_all(sent.reshape(devices, tiles, 2, LANES), ('inp', 'tm'), spl...  94.4 us
    pallas_call x1, Pallas kernels, body(): pl.pallas_call(front_kernel, in_specs=[hbm] * 3, out_specs=hbm, out_shape...  7.15 us
    pallas_call x1, Pallas kernels, body(): pl.pallas_call(lambda *refs: back_kernel(inputs // LANES, total_spectra,...  4.85 us

profile of v2, /device:TPU:1, one launch (start us, length us, event | category | flops | bytes accessed | tf_op | source)
XLA Modules:
  0.0 106.5 jit_solution(3165844804492550663)
XLA Ops:
  0.0 7.2 %shard_map.55 = bf16[5120,128]{1,0:T(8,128)(2,1)} custom-call(bf16[32,32768]{1,0:T(8,128)(2,1)} %v_hbm.1, f32[4,2048]{1,0:T(4,128)} %constant.8.clone.w_hbm, bf16[1024,512]{1,0:T(8,128)(2,1)} %constant.9.clone.t_hbm), custom_call_target="tpu_custom_call" | custom-call | tf_op jit(solution)/shard_map/pallas_call | solution.py:205
  7.2 0.0 copy-start
  7.2 0.0 copy-start.1
  7.2 94.4 %all_to_all.5 = bf16[512,5,2,128]{3,2,1,0:T(2,128)(2,1)S(1)} all-to-all(bf16[512,5,2,128]{3,2,1,0:T(2,128)(2,1)} %bitcast.3), channel_id=1, replica_groups=mesh['inp'=32,'tm'=16] {'inp','tm'}, dimensions={0} | all-to-all | bytes 2621440 | tf_op jit(solution)/shard_map/all_to_all | solution.py:224
  101.6 0.0 copy-done
  101.6 0.0 copy-done.1
  101.6 4.8 %shard_map.56 = bf16[1,1024,1024]{2,1,0:T(8,128)(2,1)} custom-call(bf16[32,160,128]{2,1,0:T(8,128)(2,1)S(1)} %bitcast.2, bf16[128,160]{1,0:T(8,128)(2,1)S(1)} %copy-done.1, bf16[512,512]{1,0:T(8,128)(2,1)S(1)} %copy-done), custom_call_target="tpu_custom_call" | custom-call | tf_op jit(solution)/shard_map/pallas_call | solution.py:232
Async XLA Ops:
  7.2 94.5 %copy-start = (bf16[512,512]{1,0:T(8,128)(2,1)S(1)}, bf16[512,512]{1,0:T(8,128)(2,1)}, u32[]{:S(2)}) copy-start(bf16[512,512]{1,0:T(8,128)(2,1)} %constant.11.clone.refs_2_) | copy-start | bytes 1572868
  7.2 94.5 %copy-start.1 = (bf16[128,160]{1,0:T(8,128)(2,1)S(1)}, bf16[128,160]{1,0:T(8,128)(2,1)}, u32[]{:S(2)}) copy-start(bf16[128,160]{1,0:T(8,128)(2,1)} %constant.10.clone.refs_1_) | copy-start | bytes 122884

commit v3 on v2

--- a/solution.py
+++ b/solution.py
@@ -28,7 +28,7 @@
     product = (bin_index[:, None] * sample[None, :]) % NFFT
     angle = (product.astype(np.float32) * np.float32(2.0 * math.pi / NFFT)).astype(np.float64)
     paired = np.stack([np.cos(angle), -np.sin(angle)]).astype(np.float32)
-    paired = paired.reshape(2, block, 4, NFFT // 4).transpose(2, 0, 1, 3)
+    paired = paired.reshape(2, block, 4, NFFT // 4).transpose(2, 0, 1, 3)[:, :, ::-1]
     return paired.reshape(2 * CHANNELS, NFFT // 4).astype(ml_dtypes.bfloat16)
 
 
@@ -91,7 +91,7 @@
             )
             for t in range(first, last):
                 for r in range(2):
-                    stage[pl.ds(residue * 2 * tiles + 2 * t + r, block, stride=8 * tiles), :] = acc[
+                    stage[pl.ds((3 - residue) * 2 * tiles + 2 * t + r, block, stride=8 * tiles), :] = acc[
                         r * block : (r + 1) * block, (t - first) * LANES : (t - first + 1) * LANES
                     ]
 
@@ -128,7 +128,7 @@
     depth = a_ref.shape[0]
     half_sign = jnp.where(lax.broadcasted_iota(jnp.int32, (1, LANES), 1) < LANES // 2, 1.0, -1.0)
     for g in range(groups):
-        joined = jnp.concatenate([x_ref[4 * g + i] for i in range(4)], axis=1)
+        joined = jnp.concatenate([x_ref[4 * groups - 1 - 4 * g - i] for i in range(4)], axis=1)
         spectra = jnp.dot(fold_ref[...], joined, preferred_element_type=jnp.float32).astype(jnp.bfloat16)
         turned = jnp.dot(spectra, perm_ref[...], preferred_element_type=jnp.float32).astype(jnp.bfloat16)
         flipped = lax.dot_general(
@@ -178,7 +178,7 @@
                 fold[r, t, u, t, u, r] = 1.0
             if t:
                 fold[r, t, 0, t - 1, tiles_local, r] = 1.0
-    return fold.reshape(2 * time_count * tiles_local, -1).astype(ml_dtypes.bfloat16)
+    return fold[:, :, :, ::-1].reshape(2 * time_count * tiles_local, -1).astype(ml_dtypes.bfloat16)
 
 
 def lane_turn():
@@ -222,7 +222,12 @@
         compiler_params=pltpu.CompilerParams(vmem_limit_bytes=60 * 1024 * 1024),
     )(voltages, jnp.asarray(filter_window()), jnp.asarray(phase_rows(block)))
     got = lax.all_to_all(
-        sent.reshape(devices, tiles, 2, LANES), ("inp", "tm"), split_axis=0, concat_axis=0, tiled=True
+        sent.reshape(devices, tiles, 2, LANES),
+        ("inp", "tm"),
+        split_axis=0,
+        concat_axis=0,
+        axis_index_groups=[list(reversed(range(devices)))],
+        tiled=True,
     )
     got = got.reshape(inp_count, time_count * tiles * 2, LANES)
     total_spectra = spec_local * time_count

time: 107 us -> 103 us (0.963)
  blocking collectives: 94.4 us -> 90.9 us
    all_to_all x1, blocking collectives: 94.4 us -> 90.9 us  [body(): lax.all_to_all(sent.reshape(devices, tiles, 2, LANES), ('inp', 'tm'), spl...]
where the time goes in v3:
time: 103 us
  blocking collectives  90.9 us (88%)
  Pallas kernels  12 us (12%)
    all_to_all x1, blocking collectives, body(): lax.all_to_all(sent.reshape(devices, tiles, 2, LANES), ('inp', 'tm'), spl...  90.9 us
    pallas_call x1, Pallas kernels, body(): pl.pallas_call(front_kernel, in_specs=[hbm] * 3, out_specs=hbm, out_shape...  7.15 us
    pallas_call x1, Pallas kernels, body(): pl.pallas_call(lambda *refs: back_kernel(inputs // LANES, total_spectra,...  4.85 us

profile of v3, /device:TPU:1, one launch (start us, length us, event | category | flops | bytes accessed | tf_op | source)
XLA Modules:
  0.0 102.9 jit_solution(13415874657406270805)
XLA Ops:
  0.0 7.1 %shard_map.55 = bf16[5120,128]{1,0:T(8,128)(2,1)} custom-call(bf16[32,32768]{1,0:T(8,128)(2,1)} %v_hbm.1, f32[4,2048]{1,0:T(4,128)} %constant.8.clone.w_hbm, bf16[1024,512]{1,0:T(8,128)(2,1)} %constant.9.clone.t_hbm), custom_call_target="tpu_custom_call" | custom-call | tf_op jit(solution)/shard_map/pallas_call | solution.py:205
  7.2 0.0 copy-start
  7.2 0.0 copy-start.1
  7.2 90.9 %all_to_all.5 = bf16[512,5,2,128]{3,2,1,0:T(2,128)(2,1)S(1)} all-to-all(bf16[512,5,2,128]{3,2,1,0:T(2,128)(2,1)} %bitcast.3), channel_id=1, replica_groups={{511,510,509,508,507,506,505,504,503,502,501,500,499,498,497,496,495,49..., dimensions={0} | all-to-all | bytes 2621440 | tf_op jit(solution)/shard_map/all_to_all | solution.py:224
  98.1 0.0 copy-done
  98.1 0.0 copy-done.1
  98.1 4.9 %shard_map.56 = bf16[1,1024,1024]{2,1,0:T(8,128)(2,1)} custom-call(bf16[32,160,128]{2,1,0:T(8,128)(2,1)S(1)} %bitcast.2, bf16[128,160]{1,0:T(8,128)(2,1)S(1)} %copy-done.1, bf16[512,512]{1,0:T(8,128)(2,1)S(1)} %copy-done), custom_call_target="tpu_custom_call" | custom-call | tf_op jit(solution)/shard_map/pallas_call | solution.py:237
Async XLA Ops:
  7.2 90.9 %copy-start = (bf16[512,512]{1,0:T(8,128)(2,1)S(1)}, bf16[512,512]{1,0:T(8,128)(2,1)}, u32[]{:S(2)}) copy-start(bf16[512,512]{1,0:T(8,128)(2,1)} %constant.11.clone.refs_2_) | copy-start | bytes 1572868
  7.2 90.9 %copy-start.1 = (bf16[128,160]{1,0:T(8,128)(2,1)S(1)}, bf16[128,160]{1,0:T(8,128)(2,1)}, u32[]{:S(2)}) copy-start(bf16[128,160]{1,0:T(8,128)(2,1)} %constant.10.clone.refs_1_) | copy-start | bytes 122884

commit v4 on v3

--- a/solution.py
+++ b/solution.py
@@ -123,26 +123,25 @@
 
 
 def back_kernel(groups, total_spectra, x_ref, fold_ref, perm_ref, out_ref, a_ref, at_ref, bt_ref, stage, sems):
-    per_group = LANES * 4
     inputs = groups * LANES
-    depth = a_ref.shape[0]
-    half_sign = jnp.where(lax.broadcasted_iota(jnp.int32, (1, LANES), 1) < LANES // 2, 1.0, -1.0)
-    for g in range(groups):
-        joined = jnp.concatenate([x_ref[4 * groups - 1 - 4 * g - i] for i in range(4)], axis=1)
-        spectra = jnp.dot(fold_ref[...], joined, preferred_element_type=jnp.float32).astype(jnp.bfloat16)
-        turned = jnp.dot(spectra, perm_ref[...], preferred_element_type=jnp.float32).astype(jnp.bfloat16)
-        flipped = lax.dot_general(
-            perm_ref[...], spectra, (((1,), (1,)), ((), ())), preferred_element_type=jnp.float32
-        )
-        swapped = pltpu.roll(flipped, LANES // 2, 1) * half_sign
-        flipped = flipped.astype(jnp.bfloat16)
-        swapped = swapped.astype(jnp.bfloat16)
-        for u in range(4):
-            rows = slice(u * LANES, (u + 1) * LANES)
-            cols = slice(g * LANES, (g + 1) * LANES)
-            a_ref[rows, cols] = turned[:, rows]
-            at_ref[cols, rows] = flipped[rows, :]
-            bt_ref[cols, rows] = swapped[rows, :]
+    half = LANES // 2
+    for h in range(groups // 2):
+        folded = []
+        for g in (2 * h, 2 * h + 1):
+            joined = jnp.concatenate([x_ref[4 * groups - 1 - 4 * g - i] for i in range(4)], axis=1)
+            spectra = jnp.dot(fold_ref[...], joined, preferred_element_type=jnp.float32)
+            folded.append(spectra.astype(jnp.bfloat16))
+        turned = jnp.dot(
+            jnp.concatenate(folded, axis=0), perm_ref[...], preferred_element_type=jnp.float32
+        ).astype(jnp.bfloat16)
+        for k in range(2):
+            cols = slice((2 * h + k) * LANES, (2 * h + k + 1) * LANES)
+            for u in range(4):
+                rows = slice(u * LANES, (u + 1) * LANES)
+                part = turned[k * LANES : (k + 1) * LANES, rows]
+                a_ref[rows, cols] = part
+                at_ref[cols, rows] = part.T
+                bt_ref[cols, rows] = jnp.concatenate([part[half:], -part[:half]], axis=0).T
     scale = 1.0 / total_spectra
     wide = a_ref[...].astype(jnp.float32)
     row_gain = lax.rsqrt(jnp.sum(wide * wide, axis=0, keepdims=True) * scale + 1e-06) * scale

time: 103 us -> 102 us (level)
  Pallas kernels: 12 us -> 10.9 us
    pallas_call x1, Pallas kernels: 4.85 us -> 3.77 us  [body(): pl.pallas_call(lambda *refs: back_kernel(inputs // LANES, total_spectra,...]
where the time goes in v4:
time: 102 us
  blocking collectives  90.9 us (89%)
  Pallas kernels  10.9 us (11%)
    all_to_all x1, blocking collectives, body(): lax.all_to_all(sent.reshape(devices, tiles, 2, LANES), ('inp', 'tm'), spl...  90.9 us
    pallas_call x1, Pallas kernels, body(): pl.pallas_call(front_kernel, in_specs=[hbm] * 3, out_specs=hbm, out_shape...  7.15 us
    pallas_call x1, Pallas kernels, body(): pl.pallas_call(lambda *refs: back_kernel(inputs // LANES, total_spectra,...  3.77 us

profile of v4, /device:TPU:1, one launch (start us, length us, event | category | flops | bytes accessed | tf_op | source)
XLA Modules:
  0.0 101.8 jit_solution(10183011562522973588)
XLA Ops:
  0.0 7.1 %shard_map.55 = bf16[5120,128]{1,0:T(8,128)(2,1)} custom-call(bf16[32,32768]{1,0:T(8,128)(2,1)} %v_hbm.1, f32[4,2048]{1,0:T(4,128)} %constant.8.clone.w_hbm, bf16[1024,512]{1,0:T(8,128)(2,1)} %constant.9.clone.t_hbm), custom_call_target="tpu_custom_call" | custom-call | tf_op jit(solution)/shard_map/pallas_call | solution.py:204
  7.2 0.0 copy-start
  7.2 0.0 copy-start.1
  7.2 90.9 %all_to_all.5 = bf16[512,5,2,128]{3,2,1,0:T(2,128)(2,1)S(1)} all-to-all(bf16[512,5,2,128]{3,2,1,0:T(2,128)(2,1)} %bitcast.3), channel_id=1, replica_groups={{511,510,509,508,507,506,505,504,503,502,501,500,499,498,497,496,495,49..., dimensions={0} | all-to-all | bytes 2621440 | tf_op jit(solution)/shard_map/all_to_all | solution.py:223
  98.1 0.0 copy-done
  98.1 0.0 copy-done.1
  98.1 3.8 %shard_map.56 = bf16[1,1024,1024]{2,1,0:T(8,128)(2,1)} custom-call(bf16[32,160,128]{2,1,0:T(8,128)(2,1)S(1)} %bitcast.2, bf16[128,160]{1,0:T(8,128)(2,1)S(1)} %copy-done.1, bf16[512,512]{1,0:T(8,128)(2,1)S(1)} %copy-done), custom_call_target="tpu_custom_call" | custom-call | tf_op jit(solution)/shard_map/pallas_call | solution.py:236
Async XLA Ops:
  7.2 90.9 %copy-start = (bf16[512,512]{1,0:T(8,128)(2,1)S(1)}, bf16[512,512]{1,0:T(8,128)(2,1)}, u32[]{:S(2)}) copy-start(bf16[512,512]{1,0:T(8,128)(2,1)} %constant.11.clone.refs_2_) | copy-start | bytes 1572868
  7.2 90.9 %copy-start.1 = (bf16[128,160]{1,0:T(8,128)(2,1)S(1)}, bf16[128,160]{1,0:T(8,128)(2,1)}, u32[]{:S(2)}) copy-start(bf16[128,160]{1,0:T(8,128)(2,1)} %constant.10.clone.refs_1_) | copy-start | bytes 122884

commit v5 on v4

--- a/solution.py
+++ b/solution.py
@@ -13,13 +13,17 @@
 CHANNELS = 512
 TAPS = 4
 LANES = 128
+WINDOW_ROWS = 512
+TABLE_ROWS = 2048
 
 
 def filter_window():
     sample = np.arange(TAPS * NFFT, dtype=np.float64) + 0.5
     shaped = np.sinc(sample / NFFT - TAPS / 2.0)
     tapered = 0.5 - 0.5 * np.cos(2.0 * math.pi * sample / (TAPS * NFFT))
-    return (shaped * tapered).reshape(TAPS, NFFT).astype(np.float32)
+    window = np.zeros((WINDOW_ROWS, NFFT), np.float32)
+    window[:TAPS] = (shaped * tapered).reshape(TAPS, NFFT)
+    return window
 
 
 def phase_rows(block):
@@ -29,10 +33,12 @@
     angle = (product.astype(np.float32) * np.float32(2.0 * math.pi / NFFT)).astype(np.float64)
     paired = np.stack([np.cos(angle), -np.sin(angle)]).astype(np.float32)
     paired = paired.reshape(2, block, 4, NFFT // 4).transpose(2, 0, 1, 3)[:, :, ::-1]
-    return paired.reshape(2 * CHANNELS, NFFT // 4).astype(ml_dtypes.bfloat16)
-
-
-def front_kernel(v_hbm, w_hbm, t_hbm, out_hbm, v_ref, w_ref, t_ref, filt, stage, packed, v_sem, w_sem, t_sem, o_sem):
+    table = np.zeros((TABLE_ROWS, NFFT // 4), ml_dtypes.bfloat16)
+    table[: 2 * CHANNELS] = paired.reshape(2 * CHANNELS, NFFT // 4).astype(ml_dtypes.bfloat16)
+    return table
+
+
+def front_kernel(v_hbm, w_hbm, t_hbm, out_ref, v_ref, w_ref, t_ref, filt, stage, v_sem, w_sem, t_sem):
     inputs = v_ref.shape[0]
     spec_local = v_ref.shape[1] // NFFT
     per_tile = LANES // inputs
@@ -46,8 +52,8 @@
         )
         for i in range(parts)
     ]
-    fetch_w = pltpu.make_async_copy(w_hbm, w_ref, w_sem)
-    fetch_t = pltpu.make_async_copy(t_hbm, t_ref, t_sem)
+    fetch_w = pltpu.make_async_copy(w_hbm.at[: w_ref.shape[0]], w_ref, w_sem)
+    fetch_t = pltpu.make_async_copy(t_hbm.at[: t_ref.shape[0]], t_ref, t_sem)
     fetch_w.start()
     fetch_v[0].start()
     fetch_v[1].start()
@@ -111,15 +117,7 @@
     for q in range(NFFT // LANES):
         filter_tiles(4, tiles, q * LANES)
     transform(2, tiles)
-    size = packed.shape[0] // 4
-    stores = []
-    for i in range(4):
-        rows = slice(i * size, (i + 1) * size)
-        packed[rows, :] = stage[rows, :].astype(jnp.bfloat16)
-        stores.append(pltpu.make_async_copy(packed.at[rows, :], out_hbm.at[rows, :], o_sem.at[i]))
-        stores[-1].start()
-    for store in stores:
-        store.wait()
+    out_ref[...] = stage[...].astype(jnp.bfloat16)
 
 
 def back_kernel(groups, total_spectra, x_ref, fold_ref, perm_ref, out_ref, a_ref, at_ref, bt_ref, stage, sems):
@@ -204,21 +202,19 @@
     sent = pl.pallas_call(
         front_kernel,
         in_specs=[hbm] * 3,
-        out_specs=hbm,
+        out_specs=pl.BlockSpec(memory_space=pltpu.VMEM),
         out_shape=jax.ShapeDtypeStruct((rows, LANES), jnp.bfloat16),
         scratch_shapes=[
             pltpu.VMEM(voltages.shape, jnp.bfloat16),
-            pltpu.VMEM((TAPS, NFFT), jnp.float32),
+            pltpu.VMEM((8, NFFT), jnp.float32),
             pltpu.VMEM((2 * CHANNELS, NFFT // 4), jnp.bfloat16),
             pltpu.VMEM((slots * local_inputs, NFFT), jnp.bfloat16),
             pltpu.VMEM((rows, LANES), jnp.float32),
-            pltpu.VMEM((rows, LANES), jnp.bfloat16),
             pltpu.SemaphoreType.DMA((4,)),
             pltpu.SemaphoreType.DMA,
             pltpu.SemaphoreType.DMA,
-            pltpu.SemaphoreType.DMA((4,)),
         ],
-        compiler_params=pltpu.CompilerParams(vmem_limit_bytes=60 * 1024 * 1024),
+        compiler_params=pltpu.CompilerParams(vmem_limit_bytes=51 * 1024 * 1024),
     )(voltages, jnp.asarray(filter_window()), jnp.asarray(phase_rows(block)))
     got = lax.all_to_all(
         sent.reshape(devices, tiles, 2, LANES),

time: 102 us -> 101 us (level)
  no operation moved by 1% of the time
where the time goes in v5:
time: 101 us
  blocking collectives  90.6 us (90%)
  Pallas kernels  10 us (10%)
    all_to_all x1, blocking collectives, body(): lax.all_to_all(sent.reshape(devices, tiles, 2, LANES), ('inp', 'tm'), spl...  90.6 us
    pallas_call x1, Pallas kernels, body(): pl.pallas_call(front_kernel, in_specs=[hbm] * 3, out_specs=pl.BlockSpec(m...  6.24 us
    pallas_call x1, Pallas kernels, body(): pl.pallas_call(lambda *refs: back_kernel(inputs // LANES, total_spectra,...  3.78 us

profile of v5, /device:TPU:1, one launch (start us, length us, event | category | flops | bytes accessed | tf_op | source)
XLA Modules:
  0.0 100.7 jit_solution(219233829927734332)
XLA Ops:
  0.0 6.2 %shard_map.55 = bf16[5120,128]{1,0:T(8,128)(2,1)S(1)} custom-call(bf16[32,32768]{1,0:T(8,128)(2,1)} %v_hbm.1, f32[512,2048]{1,0:T(8,128)} %constant.8.clone.w_hbm, bf16[2048,512]{1,0:T(8,128)(2,1)} %constant.9.clone.t_hbm), custom_call_target="tpu_custom_call" | custom-call | tf_op jit(solution)/shard_map/pallas_call | solution.py:202
  6.2 0.0 copy-start
  6.3 0.0 copy-start.1
  6.3 90.6 %all_to_all.5 = bf16[512,5,2,128]{3,2,1,0:T(2,128)(2,1)S(1)} all-to-all(bf16[512,5,2,128]{3,2,1,0:T(2,128)(2,1)S(1)} %bitcast.2), channel_id=1, replica_groups={{511,510,509,508,507,506,505,504,503,502,501,500,499,498,497,496,495,49..., dimensions={0} | all-to-all | bytes 2621440 | tf_op jit(solution)/shard_map/all_to_all | solution.py:219
  96.9 0.0 copy-done
  96.9 0.0 copy-done.1
  96.9 3.8 %shard_map.56 = bf16[1,1024,1024]{2,1,0:T(8,128)(2,1)} custom-call(bf16[32,160,128]{2,1,0:T(8,128)(2,1)S(1)} %bitcast.3, bf16[128,160]{1,0:T(8,128)(2,1)S(1)} %copy-done.1, bf16[512,512]{1,0:T(8,128)(2,1)S(1)} %copy-done), custom_call_target="tpu_custom_call" | custom-call | tf_op jit(solution)/shard_map/pallas_call | solution.py:232
Async XLA Ops:
  6.2 90.7 %copy-start = (bf16[512,512]{1,0:T(8,128)(2,1)S(1)}, bf16[512,512]{1,0:T(8,128)(2,1)}, u32[]{:S(2)}) copy-start(bf16[512,512]{1,0:T(8,128)(2,1)} %constant.11.clone.refs_2_) | copy-start | bytes 1572868
  6.3 90.7 %copy-start.1 = (bf16[128,160]{1,0:T(8,128)(2,1)S(1)}, bf16[128,160]{1,0:T(8,128)(2,1)}, u32[]{:S(2)}) copy-start(bf16[128,160]{1,0:T(8,128)(2,1)} %constant.10.clone.refs_1_) | copy-start | bytes 122884

commit v6 on v5

--- a/solution.py
+++ b/solution.py
@@ -88,18 +88,19 @@
         return jnp.concatenate([jnp.concatenate([part[r] for part in quarters], axis=1) for r in range(2)], axis=0)
 
     def transform(first, last):
-        for residue in range(4):
+        for residue in range(0, 4, 2):
             acc = lax.dot_general(
-                phases(residue),
+                jnp.concatenate([phases(residue + d) for d in range(2)], axis=0),
                 filt[first * LANES : last * LANES, :],
                 (((1,), (1,)), ((), ())),
                 preferred_element_type=jnp.float32,
             )
-            for t in range(first, last):
-                for r in range(2):
-                    stage[pl.ds((3 - residue) * 2 * tiles + 2 * t + r, block, stride=8 * tiles), :] = acc[
-                        r * block : (r + 1) * block, (t - first) * LANES : (t - first + 1) * LANES
-                    ]
+            for d in range(2):
+                for t in range(first, last):
+                    for r in range(2):
+                        stage[pl.ds((3 - residue - d) * 2 * tiles + 2 * t + r, block, stride=8 * tiles), :] = acc[
+                            (2 * d + r) * block : (2 * d + r + 1) * block, (t - first) * LANES : (t - first + 1) * LANES
+                        ]
 
     fetch_v[0].wait()
     fetch_v[1].wait()

time: 101 us -> 101 us (level)
  no operation moved by 1% of the time
where the time goes in v6:
time: 101 us; the launch traced here: 100 us
  blocking collectives  90.6 us (90%)
  Pallas kernels  9.62 us (10%)
    all_to_all x1, blocking collectives, body(): lax.all_to_all(sent.reshape(devices, tiles, 2, LANES), ('inp', 'tm'), spl...  90.6 us
    pallas_call x1, Pallas kernels, body(): pl.pallas_call(front_kernel, in_specs=[hbm] * 3, out_specs=pl.BlockSpec(m...  5.84 us
    pallas_call x1, Pallas kernels, body(): pl.pallas_call(lambda *refs: back_kernel(inputs // LANES, total_spectra,...  3.78 us

profile of v6, /device:TPU:1, one launch (start us, length us, event | category | flops | bytes accessed | tf_op | source)
XLA Modules:
  0.0 100.3 jit_solution(2829568372599739378)
XLA Ops:
  0.0 5.8 %shard_map.55 = bf16[5120,128]{1,0:T(8,128)(2,1)S(1)} custom-call(bf16[32,32768]{1,0:T(8,128)(2,1)} %v_hbm.1, f32[512,2048]{1,0:T(8,128)} %constant.8.clone.w_hbm, bf16[2048,512]{1,0:T(8,128)(2,1)} %constant.9.clone.t_hbm), custom_call_target="tpu_custom_call" | custom-call | tf_op jit(solution)/shard_map/pallas_call | solution.py:203
  5.9 0.0 copy-start
  5.9 0.0 copy-start.1
  5.9 90.6 %all_to_all.5 = bf16[512,5,2,128]{3,2,1,0:T(2,128)(2,1)S(1)} all-to-all(bf16[512,5,2,128]{3,2,1,0:T(2,128)(2,1)S(1)} %bitcast.2), channel_id=1, replica_groups={{511,510,509,508,507,506,505,504,503,502,501,500,499,498,497,496,495,49..., dimensions={0} | all-to-all | bytes 2621440 | tf_op jit(solution)/shard_map/all_to_all | solution.py:220
  96.5 0.0 copy-done
  96.5 0.0 copy-done.1
  96.5 3.8 %shard_map.56 = bf16[1,1024,1024]{2,1,0:T(8,128)(2,1)} custom-call(bf16[32,160,128]{2,1,0:T(8,128)(2,1)S(1)} %bitcast.3, bf16[128,160]{1,0:T(8,128)(2,1)S(1)} %copy-done.1, bf16[512,512]{1,0:T(8,128)(2,1)S(1)} %copy-done), custom_call_target="tpu_custom_call" | custom-call | tf_op jit(solution)/shard_map/pallas_call | solution.py:233
Async XLA Ops:
  5.9 90.7 %copy-start = (bf16[512,512]{1,0:T(8,128)(2,1)S(1)}, bf16[512,512]{1,0:T(8,128)(2,1)}, u32[]{:S(2)}) copy-start(bf16[512,512]{1,0:T(8,128)(2,1)} %constant.11.clone.refs_2_) | copy-start | bytes 1572868
  5.9 90.7 %copy-start.1 = (bf16[128,160]{1,0:T(8,128)(2,1)S(1)}, bf16[128,160]{1,0:T(8,128)(2,1)}, u32[]{:S(2)}) copy-start(bf16[128,160]{1,0:T(8,128)(2,1)} %constant.10.clone.refs_1_) | copy-start | bytes 122884

commit v7 on v6

--- a/solution.py
+++ b/solution.py
@@ -124,17 +124,17 @@
 def back_kernel(groups, total_spectra, x_ref, fold_ref, perm_ref, out_ref, a_ref, at_ref, bt_ref, stage, sems):
     inputs = groups * LANES
     half = LANES // 2
-    for h in range(groups // 2):
+    for h in range(groups // 4):
         folded = []
-        for g in (2 * h, 2 * h + 1):
+        for g in range(4 * h, 4 * h + 4):
             joined = jnp.concatenate([x_ref[4 * groups - 1 - 4 * g - i] for i in range(4)], axis=1)
             spectra = jnp.dot(fold_ref[...], joined, preferred_element_type=jnp.float32)
             folded.append(spectra.astype(jnp.bfloat16))
         turned = jnp.dot(
             jnp.concatenate(folded, axis=0), perm_ref[...], preferred_element_type=jnp.float32
         ).astype(jnp.bfloat16)
-        for k in range(2):
-            cols = slice((2 * h + k) * LANES, (2 * h + k + 1) * LANES)
+        for k in range(4):
+            cols = slice((4 * h + k) * LANES, (4 * h + k + 1) * LANES)
             for u in range(4):
                 rows = slice(u * LANES, (u + 1) * LANES)
                 part = turned[k * LANES : (k + 1) * LANES, rows]

time: 101 us -> 101 us (level)
  no operation moved by 1% of the time
where the time goes in v7:
time: 101 us; the launch traced here: 100 us
  blocking collectives  90.6 us (90%)
  Pallas kernels  9.37 us (9%)
    all_to_all x1, blocking collectives, body(): lax.all_to_all(sent.reshape(devices, tiles, 2, LANES), ('inp', 'tm'), spl...  90.6 us
    pallas_call x1, Pallas kernels, body(): pl.pallas_call(front_kernel, in_specs=[hbm] * 3, out_specs=pl.BlockSpec(m...  5.84 us
    pallas_call x1, Pallas kernels, body(): pl.pallas_call(lambda *refs: back_kernel(inputs // LANES, total_spectra,...  3.53 us

profile of v7, /device:TPU:1, one launch (start us, length us, event | category | flops | bytes accessed | tf_op | source)
XLA Modules:
  0.0 100.1 jit_solution(13530400376733681028)
XLA Ops:
  0.0 5.8 %shard_map.55 = bf16[5120,128]{1,0:T(8,128)(2,1)S(1)} custom-call(bf16[32,32768]{1,0:T(8,128)(2,1)} %v_hbm.1, f32[512,2048]{1,0:T(8,128)} %constant.8.clone.w_hbm, bf16[2048,512]{1,0:T(8,128)(2,1)} %constant.9.clone.t_hbm), custom_call_target="tpu_custom_call" | custom-call | tf_op jit(solution)/shard_map/pallas_call | solution.py:203
  5.9 0.0 copy-start
  5.9 0.0 copy-start.1
  5.9 90.6 %all_to_all.5 = bf16[512,5,2,128]{3,2,1,0:T(2,128)(2,1)S(1)} all-to-all(bf16[512,5,2,128]{3,2,1,0:T(2,128)(2,1)S(1)} %bitcast.2), channel_id=1, replica_groups={{511,510,509,508,507,506,505,504,503,502,501,500,499,498,497,496,495,49..., dimensions={0} | all-to-all | bytes 2621440 | tf_op jit(solution)/shard_map/all_to_all | solution.py:220
  96.5 0.0 copy-done
  96.5 0.0 copy-done.1
  96.5 3.5 %shard_map.56 = bf16[1,1024,1024]{2,1,0:T(8,128)(2,1)} custom-call(bf16[32,160,128]{2,1,0:T(8,128)(2,1)S(1)} %bitcast.3, bf16[128,160]{1,0:T(8,128)(2,1)S(1)} %copy-done.1, bf16[512,512]{1,0:T(8,128)(2,1)S(1)} %copy-done), custom_call_target="tpu_custom_call" | custom-call | tf_op jit(solution)/shard_map/pallas_call | solution.py:233
Async XLA Ops:
  5.9 90.7 %copy-start = (bf16[512,512]{1,0:T(8,128)(2,1)S(1)}, bf16[512,512]{1,0:T(8,128)(2,1)}, u32[]{:S(2)}) copy-start(bf16[512,512]{1,0:T(8,128)(2,1)} %constant.11.clone.refs_2_) | copy-start | bytes 1572868
  5.9 90.7 %copy-start.1 = (bf16[128,160]{1,0:T(8,128)(2,1)S(1)}, bf16[128,160]{1,0:T(8,128)(2,1)}, u32[]{:S(2)}) copy-start(bf16[128,160]{1,0:T(8,128)(2,1)} %constant.10.clone.refs_1_) | copy-start | bytes 122884
